TPU v7x, 32 devices: a whole 2x2x4 slice. The times are simulated.
32 devices in a mesh: sect: 2 (over y), node: 4 (over z), fn: 2 (over x), sub: 2 (over core).
Axes of the slice: x: 2, y: 2, z: 4, core: 2. Of those that a mesh axis runs over, the one named last changes fastest.
Arguments:
- volume_grad: bfloat16 [2048, 32, 128], P(('sect', 'node', 'fn', 'sub')), parts along dimension 0, may hold values from -0.5 to 0.5
- volume_coords: float32 [2048, 3, 128], P(('sect', 'node', 'fn', 'sub')), parts along dimension 0, may hold values from -2.1366198 to 3
- support: int32 [2048, 32], P(('sect', 'node', 'fn', 'sub')), parts along dimension 0, may hold values from 0 to 31
- control_coords: float32 [64, 3, 128], P(('sect', 'node')), parts along dimension 0, may hold values from -2.1366198 to 3
- neighbours: int32 [64, 4], P(('sect', 'node')), parts along dimension 0, may hold values from 0 to 31
- block_inverse: float32 [64, 128, 128], P(('sect', 'node')), parts along dimension 0, may hold values from -0.09375 to 0.09375
Outputs:
- control_gradient: float32 [64, 32, 128], P(('sect', 'node')), parts along dimension 0
- adjoint: float32 [64, 32, 128], P(('sect', 'node')), parts along dimension 0
There are 2 independent parts, one for each index of `sect`. A program takes and returns all parts, laid end to end along the dimension named above; each array names one. Nothing has to cross between parts.
All inputs are finite; a program needn't handle non-finite values.
Results may differ from a plain program's by a relative error of at most 0.0034.
Values may be sent and summed in bfloat16 or wider, within the bound.
A program may use at most 64 MiB of HBM per device.

v0:
```python
import jax
import jax.numpy as jnp
from jax import lax
from jax.sharding import PartitionSpec as P

SWEEPS = 2
RADIUS = 1.2


def wendland(points, centers):
    diff = points[..., :, :, None] - centers[..., :, None, :]
    dist = jnp.sqrt(jnp.sum(diff * diff, axis=-3))
    ratio = dist / RADIUS
    inside = jnp.maximum(1.0 - ratio, 0.0)
    return (inside**4 * (4.0 * ratio + 1.0)).astype(jnp.bfloat16)


def local(volume_grad, volume_coords, support, control_coords, neighbours, block_inverse):
    all_centers = lax.all_gather(control_coords, "node", axis=0, tiled=True)
    blocks = volume_grad.shape[0]
    funcs = volume_grad.shape[1]
    width = volume_grad.shape[2]
    listed = support.shape[1]
    group = 2
    count = blocks // group
    grads = volume_grad.reshape(count, group, funcs, width)
    coords = volume_coords.reshape(count, group, 3, width)
    lists = support.reshape(count, group, listed)

    def step(total, items):
        block_grads, block_coords, block_lists = items
        centers = all_centers[block_lists]
        tiles_phi = wendland(block_coords[:, None], centers)
        tiles = jnp.einsum(
            "gfi,gkij->gkfj", block_grads, tiles_phi, preferred_element_type=jnp.float32
        )
        total = total.at[block_lists.reshape(-1)].add(tiles.reshape(-1, funcs, width))
        return (total, None)

    empty = jnp.zeros((all_centers.shape[0], funcs, width), jnp.float32)
    partial_value, _ = lax.scan(step, empty, (grads, coords, lists))
    owned = lax.psum_scatter(partial_value, "node", scatter_dimension=0, tiled=True)
    control_gradient = lax.psum(owned, ("fn", "sub"))
    adjoint = jnp.einsum(
        "cfi,cij->cfj", control_gradient, block_inverse, precision=lax.Precision.HIGHEST
    )
    pair_phi = wendland(all_centers[neighbours], control_coords[:, None])
    for sweep in range(SWEEPS):
        values = lax.all_gather(adjoint.astype(jnp.bfloat16), "node", axis=0, tiled=True)
        near = values[neighbours]
        coupling = jnp.einsum("ckfi,ckij->cfj", near, pair_phi, preferred_element_type=jnp.float32)
        adjoint = jnp.einsum(
            "cfi,cij->cfj",
            control_gradient - coupling,
            block_inverse,
            precision=lax.Precision.HIGHEST,
        )
    return (control_gradient, adjoint)


def solution(mesh):
    return jax.shard_map(
        local,
        mesh=mesh,
        in_specs=(
            P(("sect", "node", "fn", "sub"), None, None),
            P(("sect", "node", "fn", "sub"), None, None),
            P(("sect", "node", "fn", "sub"), None),
            P(("sect", "node"), None, None),
            P(("sect", "node"), None),
            P(("sect", "node"), None, None),
        ),
        out_specs=(P(("sect", "node"), None, None), P(("sect", "node"), None, None)),
        check_vma=False,
    )
```

profile of v0, /device:TPU:0, one launch (start us, length us, event | category | flops | bytes accessed | tf_op | source)
XLA Modules:
  0.0 401.6 jit_solution(12092101449089686073)
XLA Ops:
  9.0 15.0 %all_gather.9 = f32[32,3,128]{2,0,1:T(8,128)S(1)} all-gather(f32[8,3,128]{2,0,1:T(8,128)} %param.11), channel_id=1, replica_groups=mesh['sect'=2,'node'=4,'fn'=2,'sub'=2] {'node'}, dimensions={0}, use_global_device_ids=true | all-gather | bytes 61440 | tf_op jit(solution)/shard_map/all_gather | solution.py:19
  24.1 280.2 %while.12 = (s32[]{:T(128)}, f32[32,32,128]{2,1,0:T(8,128)S(1)}, s32[32,2,32]{2,1,0:T(2,128)S(1)}, f32[32,2,3,128]{3,2,1,0:T(4,128)S(1)}, f32[32,3,128]{2,1,0:T(...) while((s32[]{:T(128)}, f32[32,32,128]{2,1,0:T(8,128)S(1)}, s32[32,2,32]{2,1,0:T(2,128)S(1)}, ...), condition=%wide.region_3.4_spmd, body=%wide.region_0.3_spmd.sunk | while | flops 85198208 | bytes 12910689 | solution.py:41
  29.7 3.1 scatter_fusion
  38.5 3.1 scatter_fusion
  47.2 3.1 scatter_fusion
  53.0 3.0 fusion.27
  56.0 3.1 scatter_fusion
  64.8 3.1 scatter_fusion
  73.5 3.1 scatter_fusion
  82.3 3.1 scatter_fusion
  88.0 3.0 fusion.27
  91.0 3.1 scatter_fusion
  96.7 3.0 fusion.27
  99.8 3.1 scatter_fusion
  108.5 3.1 scatter_fusion
  117.3 3.1 scatter_fusion
  123.0 3.0 fusion.27
  126.0 3.1 scatter_fusion
  131.8 3.0 fusion.27
  134.8 3.1 scatter_fusion
  143.6 3.1 scatter_fusion
  152.3 3.1 scatter_fusion
  161.1 3.1 scatter_fusion
  169.8 3.1 scatter_fusion
  178.6 3.1 scatter_fusion
  187.3 3.1 scatter_fusion
  196.1 3.1 scatter_fusion
  204.8 3.1 scatter_fusion
  210.6 3.0 fusion.27
  213.6 3.1 scatter_fusion
  219.3 3.0 fusion.27
  222.4 3.1 scatter_fusion
  228.1 3.0 fusion.27
  231.1 3.1 scatter_fusion
  236.8 3.0 fusion.27
  239.9 3.1 scatter_fusion
  248.6 3.1 scatter_fusion
  257.4 3.1 scatter_fusion
  266.1 3.1 scatter_fusion
  274.9 3.1 scatter_fusion
  283.7 3.1 scatter_fusion
  292.4 3.1 scatter_fusion
  301.2 3.1 scatter_fusion
  306.0 3.4 multiply_reduce_fusion.1
  309.4 18.7 %reduce-scatter.2.cloned.1.call-done = f32[8,32,128]{2,1,0:T(8,128)} async-done(((f32[32,32,128]{2,1,0:T(8,128)}), f32[8,32,128]{2,1,0:T(8,128)}) %reduce-scatter.2.cloned.1.call-update) | async-done | bytes 131088 | tf_op jit(solution)/shard_map/reduce_scatter | solution.py:42
  330.8 29.3 %all-reduce.2.cloned.1.call-done = f32[8,32,128]{2,1,0:T(8,128)} async-done(((f32[8,32,128]{2,1,0:T(8,128)}), f32[8,32,128]{2,1,0:T(8,128)}) %all-reduce.2.cloned.1.call-update) | async-done | bytes 131088 | tf_op jit(solution)/shard_map/psum | solution.py:43
  361.7 13.9 %all_gather.10 = bf16[32,32,128]{2,1,0:T(8,128)(2,1)S(1)} all-gather(bf16[8,32,128]{2,1,0:T(8,128)(2,1)S(1)} %convolution_convert_fusion.1), channel_id=1, replica_groups=mesh['sect'=2,'node'=4,'fn'=2,'sub'=2] {'node'}, dimensions={0}, use_global_device_ids=true | all-gather | bytes 327680 | tf_op jit(solution)/shard_map/all_gather | solution.py:49
  377.9 14.1 %all_gather.11 = bf16[32,32,128]{2,1,0:T(8,128)(2,1)S(1)} all-gather(bf16[8,32,128]{2,1,0:T(8,128)(2,1)S(1)} %convolution_convert_fusion), channel_id=1, replica_groups=mesh['sect'=2,'node'=4,'fn'=2,'sub'=2] {'node'}, dimensions={0}, use_global_device_ids=true | all-gather | bytes 327680 | tf_op jit(solution)/shard_map/all_gather | solution.py:49
  (312 shorter events, 164.1 us)
Async XLA Ops:
  7.2 353.0 %copy-start = (f32[8,128,128]{2,1,0:T(8,128)S(1)}, f32[8,128,128]{2,1,0:T(8,128)}, u32[]{:S(2)}) copy-start(f32[8,128,128]{2,1,0:T(8,128)} %param.13) | copy-start | bytes 1572868
  7.2 321.0 %reduce-scatter.2.cloned.1.call-start = ((), (), s32[]{:S(2)}) async-start(), calls=%async_computation.1 | async-start | bytes 655360 | tf_op jit(solution)/shard_map/reduce_scatter | solution.py:42
  24.1 281.1 %copy-start.3 = (f32[8,3,128]{2,0,1:T(8,128)S(1)}, f32[8,3,128]{2,0,1:T(8,128)}, u32[]{:S(2)}) copy-start(f32[8,3,128]{2,0,1:T(8,128)} %param.11) | copy-start | bytes 36868
  24.1 281.1 %copy-start.4 = (s32[8,4]{0,1:T(4,128)S(1)}, s32[8,4]{0,1:T(4,128)}, u32[]{:S(2)}) copy-start(s32[8,4]{0,1:T(4,128)} %param.12) | copy-start | bytes 388
  304.3 0.8 copy-start.1
  305.1 55.0 %all-reduce.2.cloned.1.call-start = ((), (), s32[]{:S(2)}) async-start(), calls=%async_computation.2 | async-start | bytes 262144 | tf_op jit(solution)/shard_map/psum | solution.py:43
  360.1 32.5 %copy-start.2 = (f32[8,32,128]{2,1,0:T(8,128)S(1)}, f32[8,32,128]{2,1,0:T(8,128)}, u32[]{:S(2)}) copy-start(f32[8,32,128]{2,1,0:T(8,128)} %all-reduce.2.cloned.1.call-done) | copy-start | bytes 393220
Sparse Core Ops, SparseCore 0:
  305.3 22.8 reduce-scatter.1
  330.5 29.6 all-reduce.1
where the time goes:
time: 405 us; the launch traced here: 402 us
  other arithmetic  161 us (40%)
  matrix products  102 us (25%)
  waiting for transfers between devices  48 us (12%)
  blocking collectives  42.9 us (11%)
  local copies, waits for them, and re-layouts  31.8 us (8%)
  between operations  14.2 us (4%)
    scatter-add x32, other arithmetic, step(): total.at[block_lists.reshape(-1)].add(tiles.reshape(-1, funcs, width))  100 us
    dot_general x32, matrix products, step(): jnp.einsum('gfi,gkij->gkfj', block_grads, tiles_phi, preferred_element_ty...  97 us
    reduce_sum x33, other arithmetic, wendland(): dist = jnp.sqrt(jnp.sum(diff * diff, axis=-3))  57.5 us
    psum x1, waiting for transfers between devices, local(): control_gradient = lax.psum(owned, ('fn', 'sub'))  29.3 us
    all_gather x2, blocking collectives, local(): lax.all_gather(adjoint.astype(jnp.bfloat16), 'node', axis=0, tiled=True)  28 us
    gather x32, local copies, waits for them, and re-layouts, step(): centers = all_centers[block_lists]  21 us
    reduce_scatter x1, waiting for transfers between devices, local(): lax.psum_scatter(partial_value, 'node', scatter_dimension=0, tiled=True)  18.7 us
    all_gather x1, blocking collectives, local(): all_centers = lax.all_gather(control_coords, 'node', axis=0, tiled=True)  15 us
  transfers between devices with their start and end apart: 2, of which 2 were waited for; matrix products, arithmetic and copies ran while one was open for 2% of the time, Pallas kernels for 0%

commit v1 on v0

--- a/solution.py
+++ b/solution.py
@@ -40,7 +40,7 @@
     empty = jnp.zeros((all_centers.shape[0], funcs, width), jnp.float32)
     partial_value, _ = lax.scan(step, empty, (grads, coords, lists))
     owned = lax.psum_scatter(partial_value, "node", scatter_dimension=0, tiled=True)
-    control_gradient = lax.psum(owned, ("fn", "sub"))
+    control_gradient = jnp.sum(lax.all_gather(owned, ("fn", "sub")), axis=0)
     adjoint = jnp.einsum(
         "cfi,cij->cfj", control_gradient, block_inverse, precision=lax.Precision.HIGHEST
     )

time: 405 us -> 378 us (0.933)
  waiting for transfers between devices: 48 us -> 19 us
  blocking collectives: 42.9 us -> 50.6 us
    psum x1 -> x0, waiting for transfers between devices: 29.3 us -> none  [local(): control_gradient = lax.psum(owned, ('fn', 'sub'))]
    all_gather x0 -> x1, blocking collectives: none -> 7.24 us  [local(): control_gradient = jnp.sum(lax.all_gather(owned, ('fn', 'sub')), axis=0)]
  transfers between devices with their start and end apart: 2 -> 1, of which waited for: 2 -> 1; matrix products, arithmetic and copies ran while one was open for 2% -> 1% of each run, Pallas kernels for 0% -> 0%
where the time goes in v1:
time: 378 us; the launch traced here: 375 us
  other arithmetic  158 us (42%)
  matrix products  99.9 us (26%)
  blocking collectives  50.6 us (13%)
  local copies, waits for them, and re-layouts  31.2 us (8%)
  waiting for transfers between devices  19 us (5%)
  between operations  14.2 us (4%)
    scatter-add x32, other arithmetic, step(): total.at[block_lists.reshape(-1)].add(tiles.reshape(-1, funcs, width))  100 us
    dot_general x32, matrix products, step(): jnp.einsum('gfi,gkij->gkfj', block_grads, tiles_phi, preferred_element_ty...  97 us
    reduce_sum x33, other arithmetic, wendland(): dist = jnp.sqrt(jnp.sum(diff * diff, axis=-3))  56.2 us
    all_gather x2, blocking collectives, local(): lax.all_gather(adjoint.astype(jnp.bfloat16), 'node', axis=0, tiled=True)  28.4 us
    gather x32, local copies, waits for them, and re-layouts, step(): centers = all_centers[block_lists]  21 us
    reduce_scatter x1, waiting for transfers between devices, local(): lax.psum_scatter(partial_value, 'node', scatter_dimension=0, tiled=True)  19 us
    all_gather x1, blocking collectives, local(): all_centers = lax.all_gather(control_coords, 'node', axis=0, tiled=True)  15 us
  transfers between devices with their start and end apart: 1, of which 1 were waited for; matrix products, arithmetic and copies ran while one was open for 1% of the time, Pallas kernels for 0%

profile of v1, /device:TPU:0, one launch (start us, length us, event | category | flops | bytes accessed | tf_op | source)
XLA Modules:
  0.0 374.8 jit_solution(16474226288439371210)
XLA Ops:
  9.0 15.0 %all_gather.15 = f32[32,3,128]{2,0,1:T(8,128)S(1)} all-gather(f32[8,3,128]{2,0,1:T(8,128)} %param.11), channel_id=1, replica_groups=mesh['sect'=2,'node'=4,'fn'=2,'sub'=2] {'node'}, dimensions={0}, use_global_device_ids=true | all-gather | bytes 61440 | tf_op jit(solution)/shard_map/all_gather | solution.py:19
  24.1 280.2 %while.12 = (s32[]{:T(128)}, f32[32,32,128]{2,1,0:T(8,128)S(1)}, s32[32,2,32]{2,1,0:T(2,128)S(1)}, f32[32,2,3,128]{3,2,1,0:T(4,128)S(1)}, f32[32,3,128]{2,1,0:T(...) while((s32[]{:T(128)}, f32[32,32,128]{2,1,0:T(8,128)S(1)}, s32[32,2,32]{2,1,0:T(2,128)S(1)}, ...), condition=%wide.region_3.4_spmd, body=%wide.region_0.3_spmd.sunk | while | flops 85198208 | bytes 12910689 | solution.py:41
  29.7 3.1 scatter_fusion
  38.5 3.1 scatter_fusion
  44.2 3.0 fusion.27
  47.2 3.1 scatter_fusion
  53.0 3.0 fusion.27
  56.0 3.1 scatter_fusion
  64.8 3.1 scatter_fusion
  73.5 3.1 scatter_fusion
  82.3 3.1 scatter_fusion
  88.0 3.0 fusion.27
  91.0 3.1 scatter_fusion
  96.7 3.0 fusion.27
  99.8 3.1 scatter_fusion
  108.5 3.1 scatter_fusion
  117.3 3.1 scatter_fusion
  123.0 3.0 fusion.27
  126.0 3.1 scatter_fusion
  131.8 3.0 fusion.27
  134.8 3.1 scatter_fusion
  143.6 3.1 scatter_fusion
  152.3 3.1 scatter_fusion
  161.1 3.1 scatter_fusion
  169.8 3.1 scatter_fusion
  178.6 3.1 scatter_fusion
  187.3 3.1 scatter_fusion
  196.1 3.1 scatter_fusion
  204.8 3.1 scatter_fusion
  210.6 3.0 fusion.27
  213.6 3.1 scatter_fusion
  219.3 3.0 fusion.27
  222.4 3.1 scatter_fusion
  228.1 3.0 fusion.27
  231.1 3.1 scatter_fusion
  236.8 3.0 fusion.27
  239.9 3.1 scatter_fusion
  248.6 3.1 scatter_fusion
  257.4 3.1 scatter_fusion
  266.1 3.1 scatter_fusion
  274.9 3.1 scatter_fusion
  283.7 3.1 scatter_fusion
  292.4 3.1 scatter_fusion
  301.2 3.1 scatter_fusion
  309.1 19.0 %reduce-scatter.2.cloned.1.call-done = f32[8,32,128]{2,1,0:T(8,128)} async-done(((f32[32,32,128]{2,1,0:T(8,128)}), f32[8,32,128]{2,1,0:T(8,128)}) %reduce-scatter.2.cloned.1.call-update) | async-done | bytes 131088 | tf_op jit(solution)/shard_map/reduce_scatter | solution.py:42
  328.1 7.2 %all-gather = f32[32,32,128]{2,1,0:T(8,128)S(1)} all-gather(f32[8,32,128]{2,1,0:T(8,128)} %reduce-scatter.2.cloned.1.call-done), channel_id=2, replica_groups=mesh['sect'=2,'node'=4,'fn'=2,'sub'=2] {'fn','sub'}, dimensions={0}, use_global_device_ids=true | all-gather | bytes 655360 | tf_op jit(solution)/shard_map/all_gather | solution.py:43
  336.0 14.5 %all_gather.18 = bf16[32,32,128]{2,1,0:T(8,128)(2,1)S(1)} all-gather(bf16[8,32,128]{2,1,0:T(8,128)(2,1)S(1)} %convolution_convert_fusion.1), channel_id=1, replica_groups=mesh['sect'=2,'node'=4,'fn'=2,'sub'=2] {'node'}, dimensions={0}, use_global_device_ids=true | all-gather | bytes 327680 | tf_op jit(solution)/shard_map/all_gather | solution.py:49
  351.9 13.9 %all_gather.19 = bf16[32,32,128]{2,1,0:T(8,128)(2,1)S(1)} all-gather(bf16[8,32,128]{2,1,0:T(8,128)(2,1)S(1)} %convolution_convert_fusion), channel_id=1, replica_groups=mesh['sect'=2,'node'=4,'fn'=2,'sub'=2] {'node'}, dimensions={0}, use_global_device_ids=true | all-gather | bytes 327680 | tf_op jit(solution)/shard_map/all_gather | solution.py:49
  (310 shorter events, 158.9 us)
Async XLA Ops:
  7.2 328.3 %copy-start = (f32[8,128,128]{2,1,0:T(8,128)S(1)}, f32[8,128,128]{2,1,0:T(8,128)}, u32[]{:S(2)}) copy-start(f32[8,128,128]{2,1,0:T(8,128)} %param.13) | copy-start | bytes 1572868
  7.2 321.0 %reduce-scatter.2.cloned.1.call-start = ((), (), s32[]{:S(2)}) async-start(), calls=%async_computation.1 | async-start | bytes 655360 | tf_op jit(solution)/shard_map/reduce_scatter | solution.py:42
  24.1 281.0 %copy-start.3 = (f32[8,3,128]{2,0,1:T(8,128)S(1)}, f32[8,3,128]{2,0,1:T(8,128)}, u32[]{:S(2)}) copy-start(f32[8,3,128]{2,0,1:T(8,128)} %param.11) | copy-start | bytes 36868
  24.1 281.0 %copy-start.4 = (s32[8,4]{0,1:T(4,128)S(1)}, s32[8,4]{0,1:T(4,128)}, u32[]{:S(2)}) copy-start(s32[8,4]{0,1:T(4,128)} %param.12) | copy-start | bytes 388
  304.3 0.8 copy-start.1
  335.4 32.5 %copy-start.2 = (f32[8,32,128]{2,1,0:T(8,128)}, f32[8,32,128]{2,1,0:T(8,128)S(1)}, u32[]{:S(2)}) copy-start(f32[8,32,128]{2,1,0:T(8,128)S(1)} %reduce_sum.30) | copy-start | bytes 393220
Sparse Core Ops, SparseCore 0:
  305.2 22.8 reduce-scatter.1
